TPU v7x, 32 devices: a whole 2x2x4 slice. The times are simulated.
32 devices in a mesh: dp: 16 (over z, y, core), tensor: 2 (over x).
Axes of the slice: x: 2, y: 2, z: 4, core: 2. Of those that a mesh axis runs over, the one named last changes fastest.
Arguments:
- tokens: bfloat16 [8192, 1152], P(('dp', 'tensor')), may hold values from -6 to 6
- condition: bfloat16 [32, 1152], P(('dp', 'tensor')), may hold values from -6 to 6
- grid_shape: int32 [32, 2], P('dp'), may hold values from 8 to 16, as said below
- w_ada: bfloat16 [1152, 6912], replicated, may hold values from -0.1875 to 0.1875
- b_ada: bfloat16 [6912], replicated, may hold values from -3 to 3
- w_qkv: bfloat16 [1152, 3, 1152], P(None, None, 'tensor'), may hold values from -0.1875 to 0.1875
- w_out: bfloat16 [1152, 1152], P('tensor'), may hold values from -1 to 1
- w_gate_up: bfloat16 [1152, 2, 3072], P(None, None, 'tensor'), may hold values from -0.1875 to 0.1875
- w_down: bfloat16 [3072, 1152], P('tensor'), may hold values from -0.21875 to 0.21875
- cotangent: bfloat16 [8192, 1152], P(('dp', 'tensor')), may hold values from -6 to 6
Outputs:
- layer_out: bfloat16 [8192, 1152], P(('dp', 'tensor'))
- d_tokens: float32 [8192, 1152], P(('dp', 'tensor'))
- d_condition: float32 [32, 1152], P(('dp', 'tensor'))
- grad_ada: float32 [1152, 6912], P(None, ('dp', 'tensor'))
- grad_ada_bias: float32 [6912], P(('dp', 'tensor'))
- grad_qkv: float32 [1152, 3, 1152], P('dp', None, 'tensor')
- grad_out: float32 [1152, 1152], P('tensor', 'dp')
- grad_gate_up: float32 [1152, 2, 3072], P('dp', None, 'tensor')
- grad_down: float32 [3072, 1152], P('tensor', 'dp')
Inputs may be any that keep to these rules, and one draw needn't show every extreme that they name: `grid_shape`: each image's patch grid has half of 16 to 16 rows and as many columns, drawn independently; in every draw some image is 16 by 16. An image's valid tokens are the first rows times columns of its 256 slots, row by row.
All inputs are finite; a program needn't handle non-finite values.
Results may differ from a plain program's by a relative error of at most 0.029.
The roundings to bfloat16 on the way count: a program that leaves them out, or rounds other values in their place, can miss the bound.
Values may be sent and summed in bfloat16 or wider, within the bound.
A program may use at most 192 MiB of HBM per device.

v0:
```python
import functools

import jax
import jax.numpy as jnp
from jax import lax
from jax.experimental import pallas as pl
from jax.experimental.pallas import tpu as pltpu
from jax.sharding import PartitionSpec as P

HD = 72
LEN = 256
EPSILON = 1e-06
MESH = pl.DeviceIdType.MESH
F32 = jnp.float32
BF16 = jnp.bfloat16
ROWS = 32
STRIP = 384
TILE = 256


def dot(left, right, left_dim, right_dim):
    return lax.dot_general(
        left, right, (((left_dim,), (right_dim,)), ((), ())), preferred_element_type=F32
    )


def normed(values):
    centered = values - jnp.mean(values, axis=-1, keepdims=True)
    variance = jnp.mean(centered * centered, axis=-1, keepdims=True)
    inverse = lax.rsqrt(variance + EPSILON)
    return centered * inverse, inverse


def norm_back(upstream, norm, inverse):
    mean_grad = jnp.mean(upstream, axis=-1, keepdims=True)
    mean_cross = jnp.mean(upstream * norm, axis=-1, keepdims=True)
    return inverse * (upstream - mean_grad - norm * mean_cross)


def rotate_rows(values):
    quarter = HD // 4
    a, b = values[:quarter], values[quarter : 2 * quarter]
    c, d = values[2 * quarter : 3 * quarter], values[3 * quarter :]
    return jnp.concatenate([-b, a, -d, c], axis=0)


def fold(values):
    return jnp.sum(values.reshape(values.shape[0] // 8, 8, values.shape[1]), axis=0)


def block_kernel(
    plan, tok, cot, mod, cos_t, sin_t, valid,
    wqkv_hbm, wout_hbm, wgu_hbm, wdown_hbm,
    out, dtok, dmod, *rest,
):
    results, rest = rest[: plan["results"]], rest[plan["results"] :]
    (
        wqkv, wout, wg, wu, wdown,
        h1, h2, dml, dat,
        q_s, k_s, v_s, p_s, qkv_f, a_f, a_t,
        hid, dgate, dup, dqkv,
        attn, dx1, own,
        send_a, send_c, recv_a, recv_b, recv_c,
        flip, sums,
        wsem, ssem, rsem, *extra,
    ) = rest
    width = tok.shape[1]
    heads = q_s.shape[0] // 2
    head_cols = heads * HD
    inner = wdown.shape[0]
    side = lax.axis_index("tensor")
    mate = {"tensor": 1 - side}
    scale = HD ** (-0.5)

    loads = [
        pltpu.make_async_copy(src, dst, wsem.at[i])
        for i, (src, dst) in enumerate(
            (
                (wqkv_hbm, wqkv), (wout_hbm, wout), (wgu_hbm.at[0], wg), (wgu_hbm.at[1], wu),
                (wdown_hbm, wdown),
            )
        )
    ]
    for load in loads:
        load.start()

    me = lax.axis_index("dp")

    def bit_of(stride):
        return lax.rem(lax.div(me, stride), 2)

    def partner(stride):
        return {"dp": me + stride - 2 * stride * bit_of(stride)}

    barrier = pltpu.get_barrier_semaphore()
    friends = [mate] + [partner(s) for s in plan["strides"]]
    for friend in friends:
        pl.semaphore_signal(barrier, inc=1, device_id=friend, device_id_type=MESH)
    pl.semaphore_wait(barrier, len(friends))

    def give(src, dst, slot):
        return pltpu.make_async_remote_copy(
            src_ref=src, dst_ref=dst, send_sem=ssem.at[slot], recv_sem=rsem.at[slot],
            device_id=mate, device_id_type=MESH,
        )

    def gather(buf, slot):
        half = LEN // 2
        return [
            give(buf.at[0, pl.ds(c * half, half)], buf.at[1, pl.ds(c * half, half)], slot + c)
            for c in range(2)
        ]

    strips = width // STRIP

    def scatter(send, recv, slot):
        return [
            give(
                send.at[:, pl.ds(c * STRIP, STRIP)], recv.at[:, pl.ds(c * STRIP, STRIP)], slot + c
            )
            for c in range(strips)
        ]

    go_h1, go_dml, go_h2, go_dat = (gather(b, 2 * i) for i, b in enumerate((h1, dml, h2, dat)))
    go_a, go_b, go_c, go_d = (
        scatter(s, r, 8 + strips * i)
        for i, (s, r) in enumerate(
            ((send_a, recv_a), (send_a, recv_b), (send_c, recv_c), (send_a, recv_a))
        )
    )

    def rows_loop(step, copies=None):
        half = LEN // 2
        count = half // ROWS
        for c in range(2):
            def one(i, carry, c=c):
                step(pl.ds(pl.multiple_of(c * half + i * ROWS, ROWS), ROWS))
                return carry
            lax.fori_loop(0, count, one, 0)
            if copies is not None:
                copies[c].start()

    shift_one, scale_one, gate_one = mod[0:1], mod[1:2], mod[2:3]
    shift_two, scale_two, gate_two = mod[3:4], mod[4:5], mod[5:6]

    def first_norm(rows):
        norm, _ = normed(tok[rows, :].astype(F32))
        h1[0, rows, :] = (norm * (1.0 + scale_one) + shift_one).astype(BF16)

    rows_loop(first_norm, go_h1)

    def mlp_grad(rows):
        dml[0, rows, :] = (gate_two * cot[rows, :].astype(F32)).astype(BF16)

    rows_loop(mlp_grad, go_dml)
    sums[...] = jnp.zeros_like(sums)

    def heads_forward(image):
        for part in range(3):
            qkv_f[part * head_cols : (part + 1) * head_cols, :] = dot(
                wqkv[part * head_cols : (part + 1) * head_cols, :], h1[image], 1, 1
            )
        cosine, sine = cos_t[image], sin_t[image]
        ok = valid[image][:, :1] > 0.0

        def head(h, carry):
            at = image * heads + h
            rows = pl.ds(pl.multiple_of(h * HD, 8), HD)
            query = qkv_f[rows, :]
            key = qkv_f[pl.ds(pl.multiple_of(head_cols + h * HD, 8), HD), :]
            value = qkv_f[pl.ds(pl.multiple_of(2 * head_cols + h * HD, 8), HD), :].astype(BF16)
            query = ((query * cosine + rotate_rows(query) * sine) * scale).astype(BF16)
            key = (key * cosine + rotate_rows(key) * sine).astype(BF16)
            q_s[at], k_s[at], v_s[at] = query, key, value
            scores = dot(key, query, 0, 0)
            scores = jnp.where(ok, scores, -1e30)
            top = jnp.max(scores, axis=0, keepdims=True)
            exps = jnp.exp(scores - top)
            probs = exps * (1.0 / jnp.sum(exps, axis=0, keepdims=True))
            p_s[at] = probs
            a_f[rows, :] = dot(value, probs.astype(BF16), 1, 0)
            return carry

        lax.fori_loop(0, heads, head, 0)
        a_t[image] = a_f[...].astype(BF16)

    def strips_of(make, send=None, copies=None, keep=None):
        for c in range(strips):
            cols = slice(c * STRIP, (c + 1) * STRIP)
            value = make(cols)
            if send is not None:
                send[:, cols] = value.astype(BF16)
                copies[c].start()
            else:
                keep[:, cols] = value

    loads[0].wait()
    heads_forward(0)
    for copy in go_h1:
        copy.wait_recv()
    heads_forward(1)
    loads[1].wait()
    strips_of(lambda cols: dot(a_t[1], wout[:, cols], 0, 0), send_a, go_a)
    strips_of(lambda cols: dot(a_t[0], wout[:, cols], 0, 0), keep=own)
    for copy in go_a:
        copy.wait_recv()

    def second_norm(rows):
        branch = own[rows, :] + recv_a[rows, :].astype(F32)
        attn[rows, :] = branch
        middle = tok[rows, :].astype(F32) + gate_one * branch
        norm, _ = normed(middle)
        h2[0, rows, :] = (norm * (1.0 + scale_two) + shift_two).astype(BF16)

    rows_loop(second_norm, go_h2)

    for load in loads[2:]:
        load.wait()

    def feed_forward(image):
        def tile(j, carry):
            cols = pl.ds(pl.multiple_of(j * TILE, TILE), TILE)
            gate = dot(h2[image], wg[:, cols], 1, 0)
            up = dot(h2[image], wu[:, cols], 1, 0)
            grad = dot(dml[image], wdown[cols, :], 1, 1)
            sig = jax.nn.sigmoid(gate)
            act = gate * sig
            hid[image, :, cols] = (act * up).astype(BF16)
            dgate[image, :, cols] = (grad * up * sig * (1.0 + gate * (1.0 - sig))).astype(BF16)
            dup[image, :, cols] = (grad * act).astype(BF16)
            return carry

        lax.fori_loop(0, inner // TILE, tile, 0)

    for copy in go_dml:
        copy.wait_recv()
    feed_forward(0)
    for copy in go_h2:
        copy.wait_recv()
    feed_forward(1)

    def dh2_strip(image):
        return lambda cols: dot(dgate[image], wg[cols, :], 1, 1) + dot(dup[image], wu[cols, :], 1, 1)

    def mlp_strip(image):
        return lambda cols: dot(hid[image], wdown[:, cols], 1, 0)

    for copy in go_a:
        copy.wait_send()
    strips_of(dh2_strip(1), send_a, go_b)
    strips_of(mlp_strip(1), send_c, go_c)
    strips_of(dh2_strip(0), keep=own)

    def turned(left, order):
        for image in range(2):
            flat = left[image].astype(F32).T
            chunk = width // plan["count"]
            for pair in range(plan["count"] // 2):
                place = [2 * pair, 2 * pair + 1]
                parts = []
                for spot in place:
                    which = 0
                    for level, stride in enumerate(order):
                        which += stride * ((spot >> (len(order) - 1 - level)) & 1)
                    parts.append(flat[which * chunk : (which + 1) * chunk])
                flip[2 * pair * chunk : 2 * (pair + 1) * chunk, image * LEN : (image + 1) * LEN] = (
                    jnp.concatenate(parts, axis=0).astype(BF16)
                )

    if plan["fused"]:
        (give_one, land0, final, gsend, grecv, osem, credit, *spots) = extra
        many = len(plan["pieces"])
        land1, land2, land3, held3 = (spots[n * many : (n + 1) * many] for n in range(4))
        half = width // 2
        gives = [wu.at[pl.ds(half, half)], give_one]
        core_bit = bit_of(1)
        state = {"gives": 0, "lands": 0}

        class Piece:
            def __init__(self, name, order, columns, padded, keep, offset, result, at):
                self.name, self.order, self.columns, self.padded = name, order, columns, padded
                self.keep, self.offset, self.result, self.at = keep, offset, result, at
                self.index = plan["pieces"].index(name)
                self.lanes = pl.ds(offset, padded)
                self.copies = {}

            def send(self, level, src, dst):
                copy = pltpu.make_async_remote_copy(
                    src_ref=src, dst_ref=dst, send_sem=gsend.at[self.index, level],
                    recv_sem=grecv.at[self.index, level], device_id=partner(self.order[level]),
                    device_id_type=MESH,
                )
                copy.start()
                self.copies[level] = copy

            def compute(self, right, give):
                self.give = gives[give]
                step = STRIP

                def tile(start, size, pad):
                    total = right(start, size)
                    low, high = total[:half], total[half:]
                    kept = jnp.where(core_bit == 0, low, high).astype(BF16)
                    gone = jnp.where(core_bit == 0, high, low).astype(BF16)
                    place = self.offset + start
                    if pad > size:
                        blank = jnp.zeros((half, pad - size), BF16)
                        kept = jnp.concatenate([kept, blank], axis=1)
                        gone = jnp.concatenate([gone, blank], axis=1)
                    if not isinstance(start, int):
                        place = pl.multiple_of(place, 128)
                        start = pl.multiple_of(start, 128)
                    self.keep[:, pl.ds(place, pad)] = kept
                    self.give[:, pl.ds(start, pad)] = gone

                whole = self.columns // step

                def one(n, carry):
                    tile(n * step, step, step)
                    return carry

                lax.fori_loop(0, whole, one, 0)
                left = self.columns - whole * step
                if left:
                    tile(whole * step, left, self.padded - whole * step)

            def go(self):
                pl.semaphore_wait(credit, 1)
                self.send(0, self.give.at[:, pl.ds(0, self.padded)], land0.at[:, pl.ds(0, self.padded)])

            def add(self, level):
                rows = half >> level
                base = 0
                for before in range(1, level + 1):
                    base = base + bit_of(self.order[before]) * (half >> before)
                self.copies[level].wait_recv()
                cut = pl.ds(0, self.padded)
                if level == 0:
                    source = land0
                elif level == 1:
                    source = land1[self.index]
                elif level == 2:
                    source = land2[self.index]
                if level < 2:
                    block = 48

                    def one(n, carry):
                        there = pl.ds(pl.multiple_of(n * block, 16), block)
                        here = pl.ds(pl.multiple_of(base + n * block, 16), block)
                        self.keep[here, self.lanes] = (
                            self.keep[here, self.lanes].astype(F32) + source[there, cut].astype(F32)
                        ).astype(BF16)
                        return carry

                    lax.fori_loop(0, rows // block, one, 0)
                    if level == 0:
                        pl.semaphore_signal(
                            credit, inc=1, device_id=partner(1), device_id_type=MESH
                        )
                    quarter = rows // 2
                    off = pl.multiple_of(base + (1 - bit_of(self.order[level + 1])) * quarter, 16)
                    target = (land1, land2)[level][self.index]
                    self.send(level + 1, self.keep.at[pl.ds(off, quarter), self.lanes], target)
                elif level == 2:
                    here = pl.ds(pl.multiple_of(base, 16), rows)
                    total = self.keep[here, self.lanes].astype(F32) + source[:, cut].astype(F32)
                    held3[self.index][0] = total[: rows // 2].astype(BF16)
                    held3[self.index][1] = total[rows // 2 :].astype(BF16)
                    bit = bit_of(self.order[3])
                    self.send(3, held3[self.index].at[1 - bit], land3[self.index].at[0])
                else:
                    bit = bit_of(self.order[3])
                    if state.get("final") is not None:
                        state["final"].wait()
                    final[:, cut] = held3[self.index][bit].astype(F32) + land3[self.index][
                        0
                    ].astype(F32)
                    copy = pltpu.make_async_copy(
                        final.at[:, cut], self.result.at[:, pl.ds(self.at, self.padded)], osem
                    )
                    copy.start()
                    state["final"] = copy

            def close(self):
                for copy in self.copies.values():
                    copy.wait_send()

        pl.semaphore_signal(credit, inc=1, device_id=partner(1), device_id_type=MESH)
        y_first, z_first = plan["orders"]
        low, high = wg.at[pl.ds(0, half)], wg.at[pl.ds(half, half)]
        third = [wqkv.at[pl.ds(n * half, half)] for n in range(3)]
        p_down = Piece("down", y_first, inner, inner, low, 0, results[0], 0)
        p_gate = Piece("gate", y_first, inner, inner, high, 0, results[0], inner)
        p_up = Piece("up", z_first, inner, inner, wu.at[pl.ds(0, half)], 0, results[0], 2 * inner)
        qk_cols = 2 * head_cols
        v_pad = -(-head_cols // 128) * 128
        p_qk = Piece("qk", y_first, qk_cols, qk_cols, third[0], 0, results[0], 3 * inner)
        p_v = Piece("v", y_first, head_cols, v_pad, third[1], 0, results[0], 3 * inner + qk_cols)
        p_out = Piece(
            "out", y_first, head_cols, v_pad, third[2], 0, results[0], 3 * inner + qk_cols + v_pad
        )

    def lane_right(array):
        def right(start, size):
            if not isinstance(start, int):
                start = pl.multiple_of(start, 128)
            part = [array[i, :, pl.ds(start, size)] for i in range(2)]
            return dot(flip[:, 0:LEN], part[0], 1, 0) + dot(flip[:, LEN:], part[1], 1, 0)
        return right

    def row_right(array, base):
        def right(start, size):
            at = base + start
            if not isinstance(start, int):
                at = pl.multiple_of(at, 16)
            part = [array[i, pl.ds(at, size), :] for i in range(2)]
            return dot(flip[:, 0:LEN], part[0], 1, 1) + dot(flip[:, LEN:], part[1], 1, 1)
        return right

    def plain_grad(right, columns, target):
        (stage, gsem) = extra
        pend = {}
        for n, start in enumerate(range(0, columns, TILE)):
            size = min(TILE, columns - start)
            slot = n % 2
            if slot in pend:
                pend[slot].wait()
            stage[slot, :, 0:size] = right(start, size).astype(BF16)
            copy = pltpu.make_async_copy(
                stage.at[slot], target.at[:, pl.ds(start, TILE)], gsem.at[slot]
            )
            copy.start()
            pend[slot] = copy
        for copy in pend.values():
            copy.wait()

    def plain_grad_in(left, right, columns, target):
        for image in range(2):
            flip[:, image * LEN : (image + 1) * LEN] = left[image].astype(F32).T.astype(BF16)
        plain_grad(right, columns, target)

    if plan["fused"]:
        turned(dml, y_first)
        p_down.compute(lane_right(hid), 0)
        p_down.go()
        turned(h2, y_first)
        p_gate.compute(lane_right(dgate), 1)
        p_down.add(0)
        p_gate.go()
    else:
        plain_grad_in(dml, lane_right(hid), inner, results[0])
        plain_grad_in(h2, lane_right(dgate), inner, results[1])
        plain_grad_in(h2, lane_right(dup), inner, results[2])

    for copy in go_b:
        copy.wait_recv()

    def second_back(rows):
        grad = own[rows, :] + recv_b[rows, :].astype(F32)
        norm, inverse = normed(tok[rows, :].astype(F32) + gate_one * attn[rows, :])
        middle = cot[rows, :].astype(F32) + norm_back(grad * (1.0 + scale_two), norm, inverse)
        dx1[rows, :] = middle
        dat[0, rows, :] = (gate_one * middle).astype(BF16)
        sums[2] += fold(middle * attn[rows, :])
        sums[3] += fold(grad)
        sums[4] += fold(grad * norm)

    rows_loop(second_back, go_dat)

    if plan["fused"]:
        p_gate.add(0)
        p_down.copies[0].wait_send()
        turned(h2, z_first)
        p_up.compute(lane_right(dup), 0)
        p_up.go()

    def heads_back(image):
        a_f[...] = dot(wout[...], dat[image], 1, 1)
        cosine, sine = cos_t[image], sin_t[image]

        def head(h, carry):
            at = image * heads + h
            rows = pl.ds(pl.multiple_of(h * HD, 8), HD)
            da = a_f[rows, :].astype(BF16)
            probs = p_s[at]
            query, key, value = q_s[at], k_s[at], v_s[at]
            dprobs = dot(value, da, 0, 0)
            dvalue = dot(da, probs.astype(BF16), 1, 1)
            inside = jnp.sum(probs * dprobs, axis=0, keepdims=True)
            dscores = (probs * (dprobs - inside)).astype(BF16)
            dquery = dot(key, dscores, 1, 0)
            dkey = dot(query, dscores, 1, 1)
            dquery = (dquery * cosine - rotate_rows(dquery * sine)) * scale
            dkey = dkey * cosine - rotate_rows(dkey * sine)
            qkv_f[rows, :] = dquery
            qkv_f[pl.ds(pl.multiple_of(head_cols + h * HD, 8), HD), :] = dkey
            qkv_f[pl.ds(pl.multiple_of(2 * head_cols + h * HD, 8), HD), :] = dvalue
            return carry

        lax.fori_loop(0, heads, head, 0)
        dqkv[image] = qkv_f[...].astype(BF16)

    heads_back(0)
    if plan["fused"]:
        p_up.add(0)
    for copy in go_dat:
        copy.wait_recv()
    heads_back(1)

    def dh1_strip(image):
        return lambda cols: dot(dqkv[image], wqkv[:, cols], 0, 0)

    for copy in go_b:
        copy.wait_send()
    strips_of(dh1_strip(1), send_a, go_d)
    strips_of(dh1_strip(0), keep=own)

    if plan["fused"]:
        p_gate.copies[0].wait_send()
        p_up.copies[0].wait_send()
        turned(h1, y_first)
        p_qk.compute(row_right(dqkv, 0), 0)
        p_qk.go()
        p_v.compute(row_right(dqkv, 2 * head_cols), 1)
        p_qk.add(0)
        p_v.go()
        p_qk.copies[0].wait_send()
        turned(dat, y_first)
        p_out.compute(row_right(a_t, 0), 0)
        p_v.add(0)
        p_out.go()
        p_down.add(1)
        p_up.add(1)
        p_out.add(0)
    else:
        plain_grad_in(h1, row_right(dqkv, 0), 3 * head_cols, results[3])
        plain_grad_in(dat, row_right(a_t, 0), head_cols, results[4])

    for copy in go_d:
        copy.wait_recv()

    def first_back(rows):
        grad = own[rows, :] + recv_a[rows, :].astype(F32)
        norm, inverse = normed(tok[rows, :].astype(F32))
        dtok[rows, :] = dx1[rows, :] + norm_back(grad * (1.0 + scale_one), norm, inverse)
        sums[0] += fold(grad)
        sums[1] += fold(grad * norm)

    rows_loop(first_back)

    strips_of(mlp_strip(0), keep=own)
    for copy in go_c:
        copy.wait_recv()

    def finish(rows):
        branch = own[rows, :] + recv_c[rows, :].astype(F32)
        out[rows, :] = (
            tok[rows, :].astype(F32) + gate_one * attn[rows, :] + gate_two * branch
        ).astype(BF16)
        sums[5] += fold(cot[rows, :].astype(F32) * branch)

    rows_loop(finish)
    for n in range(6):
        dmod[n : n + 1, :] = jnp.sum(sums[n], axis=0, keepdims=True)
    if plan["fused"]:
        p_down.add(2)
        p_gate.add(1)
        p_down.add(3)
        p_up.add(2)
        p_qk.add(1)
        p_gate.add(2)
        p_up.add(3)
        p_v.add(1)
        p_qk.add(2)
        p_gate.add(3)
        p_out.add(1)
        p_v.add(2)
        p_qk.add(3)
        p_out.add(2)
        p_v.add(3)
        p_out.add(3)
        state["final"].wait()
        pl.semaphore_wait(credit, 1)
        for piece in (p_gate, p_up, p_qk, p_v, p_out, p_down):
            for level, copy in piece.copies.items():
                if level > 0 or piece in (p_v, p_out):
                    copy.wait_send()
    for copy in (*go_h1, *go_dml, *go_h2, *go_dat, *go_c, *go_d):
        copy.wait_send()


def run_block(tok, cot, mod, cos_t, sin_t, valid, wqkv, wout, wgu, wdown):
    width = tok.shape[1]
    head_cols = wout.shape[0]
    heads = head_cols // HD
    inner = wdown.shape[0]
    strips = width // STRIP
    count = lax.axis_size("dp")
    vmem = pl.BlockSpec(memory_space=pltpu.VMEM)
    hbm = pl.BlockSpec(memory_space=pl.ANY)
    V = pltpu.VMEM
    D = pltpu.SemaphoreType.DMA
    copies = 8 + 4 * strips
    fused = count == 16 and width % (8 * count) == 0
    names = ["down", "gate", "up", "qk", "v", "out"]
    pad = -(-head_cols // 128) * 128
    if fused:
        results = [jax.ShapeDtypeStruct((width // count, 3 * inner + 2 * head_cols + 2 * pad), F32)]
        chunk = width // count
        widths = [inner, inner, inner, 2 * head_cols, pad, pad]
        extra = [
            V((width // 2, inner), BF16),
            V((width // 2, inner), BF16),
            V((chunk, inner), F32),
            D((len(names), 4)),
            D((len(names), 4)),
            D(()),
            pltpu.SemaphoreType.REGULAR,
            *[V((width // 4, w), BF16) for w in widths],
            *[V((width // 8, w), BF16) for w in widths],
            *[V((1, chunk, w), BF16) for w in widths],
            *[V((2, chunk, w), BF16) for w in widths],
        ]
        strides = [1, 2, 4, 8]
    else:
        wide = [inner, inner, inner, 3 * head_cols, head_cols]
        results = [jax.ShapeDtypeStruct((width, -(-w // TILE) * TILE), BF16) for w in wide]
        extra = [V((2, width, TILE), BF16), D((2,))]
        strides = []
    plan = {
        "fused": fused, "results": len(results), "count": count, "pieces": names,
        "strides": strides, "orders": ((1, 2, 4, 8), (1, 4, 2, 8)),
    }
    return pl.pallas_call(
        functools.partial(block_kernel, plan),
        out_shape=(
            jax.ShapeDtypeStruct((LEN, width), BF16),
            jax.ShapeDtypeStruct((LEN, width), F32),
            jax.ShapeDtypeStruct((6, width), F32),
            *results,
        ),
        in_specs=[vmem] * 6 + [hbm] * 4,
        out_specs=[vmem] * 3 + [hbm] * len(results),
        scratch_shapes=[
            V(wqkv.shape, BF16), V(wout.shape, BF16), V(wgu.shape[1:], BF16),
            V(wgu.shape[1:], BF16), V(wdown.shape, BF16),
            *[V((2, LEN, width), BF16)] * 4,
            *[V((2 * heads, HD, LEN), BF16)] * 3,
            V((2 * heads, LEN, LEN), F32),
            V((3 * head_cols, LEN), F32),
            V((head_cols, LEN), F32),
            V((2, head_cols, LEN), BF16),
            *[V((2, LEN, inner), BF16)] * 3,
            V((2, 3 * head_cols, LEN), BF16),
            *[V((LEN, width), F32)] * 3,
            *[V((LEN, width), BF16)] * 5,
            V((width, 2 * LEN), BF16),
            V((6, 8, width), F32),
            D((5,)),
            D((copies,)),
            D((copies,)),
            *extra,
        ],
        compiler_params=pltpu.CompilerParams(
            collective_id=0, has_side_effects=True, vmem_limit_bytes=62 * 1024 * 1024
        ),
    )(tok, cot, mod, cos_t, sin_t, valid, wqkv, wout, wgu, wdown)


def rope_tables(grid_shape):
    position = jnp.arange(LEN, dtype=jnp.int32)[None, :]
    widths = grid_shape[:, 1:2]
    rows_at = position // widths
    cols_at = position % widths
    key_valid = position < grid_shape[:, 0:1] * widths
    quarter = HD // 4
    frequency = 10000.0 ** (-jnp.arange(quarter, dtype=F32) / quarter)
    row_angle = rows_at.astype(F32)[:, None, :] * frequency[:, None]
    col_angle = cols_at.astype(F32)[:, None, :] * frequency[:, None]
    angles = jnp.concatenate([row_angle, row_angle, col_angle, col_angle], axis=1)
    valid = jnp.broadcast_to(key_valid.astype(F32)[:, :, None], (*key_valid.shape, 128))
    return jnp.cos(angles), jnp.sin(angles), valid


def sum_over_images(partial):
    count = lax.axis_size("dp")
    me = lax.axis_index("dp")
    held = partial.reshape(count, partial.shape[0] // count, partial.shape[1])
    stride = 1
    left = count
    while left > 1:
        bit = (me // stride) % 2
        pairs = held.reshape(left // 2, 2, *held.shape[1:])
        keep = lax.dynamic_index_in_dim(pairs, bit, 1, keepdims=False)
        send = lax.dynamic_index_in_dim(pairs, 1 - bit, 1, keepdims=False)
        came = lax.ppermute(send, "dp", [(i, i ^ stride) for i in range(count)])
        held = keep.astype(F32) + came.astype(F32)
        left //= 2
        stride *= 2
        if left > 1:
            held = held.astype(BF16)
    return held[0]


def body(tokens, condition, grid_shape, w_ada, b_ada, w_qkv, w_out, w_gate_up, w_down, cotangent):
    width = tokens.shape[1]
    inner = w_down.shape[0]
    head_cols = w_out.shape[0]
    cond = condition.astype(F32)
    cond_sigmoid = jax.nn.sigmoid(cond)
    silu_cond = (cond * cond_sigmoid).astype(BF16)
    mod = jnp.dot(silu_cond, w_ada, preferred_element_type=F32) + b_ada.astype(F32)
    mod = mod.reshape(6, width)
    mine = lax.axis_index("tensor")
    grid_shape = jnp.where(mine == 0, grid_shape, grid_shape[::-1])
    cos_t, sin_t, valid = rope_tables(grid_shape)
    wqkv = w_qkv.transpose(1, 2, 0).reshape(3 * head_cols, width)
    layer_out, d_tokens, d_mod, *grads = run_block(
        tokens, cotangent, mod, cos_t, sin_t, valid, wqkv, w_out,
        w_gate_up.transpose(1, 0, 2), w_down,
    )
    if len(grads) == 1:
        whole = grads[0]
        pad = -(-head_cols // 128) * 128
        grad_down = whole[:, :inner].T
        grad_gate_up = whole[:, inner : 3 * inner].reshape(-1, 2, inner)
        grad_qkv = whole[:, 3 * inner : 3 * inner + 3 * head_cols].reshape(-1, 3, head_cols)
        start = 3 * inner + 2 * head_cols + pad
        grad_out = whole[:, start : start + head_cols].T
    else:
        grad_down = sum_over_images(grads[0]).T
        grad_gate_up = jnp.stack([sum_over_images(grads[1]), sum_over_images(grads[2])], axis=1)
        grad_qkv = sum_over_images(grads[3][:, : 3 * head_cols]).reshape(-1, 3, head_cols)
        grad_out = sum_over_images(grads[4][:, :head_cols]).T
    d_mod = d_mod.reshape(1, 6 * width).astype(BF16)
    d_condition = (
        dot(d_mod, w_ada, 1, 1) * cond_sigmoid * (1.0 + cond * (1.0 - cond_sigmoid))
    )
    devices_all = lax.axis_size("dp") * lax.axis_size("tensor")
    own_cols = 6 * width // devices_all
    packed = jnp.concatenate(
        [
            d_mod.reshape(devices_all, own_cols),
            jnp.broadcast_to(silu_cond, (devices_all, width)),
        ],
        axis=1,
    )
    packed = jnp.pad(packed, ((0, 0), (0, -packed.shape[1] % 128)))
    packed = lax.all_to_all(
        packed.reshape(devices_all, -1, 128), ("dp", "tensor"), 0, 0, tiled=True
    ).reshape(devices_all, -1)
    columns = packed[:, :own_cols]
    silu_rows = packed[:, own_cols : own_cols + width]
    weight_part = dot(silu_rows, columns, 0, 0)
    bias_part = jnp.sum(columns.astype(F32), axis=0)
    return (
        layer_out, d_tokens, d_condition, weight_part, bias_part,
        grad_qkv, grad_out, grad_gate_up, grad_down,
    )


def solution(mesh):
    placed = (
        P(("dp", "tensor"), None),
        P(("dp", "tensor"), None),
        P("dp", None),
        P(),
        P(),
        P(None, None, "tensor"),
        P("tensor", None),
        P(None, None, "tensor"),
        P("tensor", None),
        P(("dp", "tensor"), None),
    )
    return jax.shard_map(
        body,
        mesh=mesh,
        in_specs=placed,
        out_specs=(
            P(("dp", "tensor"), None),
            P(("dp", "tensor"), None),
            P(("dp", "tensor"), None),
            P(None, ("dp", "tensor")),
            P(("dp", "tensor")),
            P("dp", None, "tensor"),
            P("tensor", "dp"),
            P("dp", None, "tensor"),
            P("tensor", "dp"),
        ),
        check_vma=False,
    )
```

profile of v0, /device:TPU:0, one launch (start us, length us, event | category | flops | bytes accessed | tf_op | source)
XLA Modules:
  0.0 238.7 jit_solution(7262868231000321061)
XLA Ops:
  0.6 0.7 rev.3
  1.3 0.7 broadcast_select_fusion
  2.0 0.2 multiply_reduce_fusion
  2.2 0.2 compare_reduce_fusion
  2.5 0.1 compare_convert_fusion
  2.5 0.0 copy-start.2
  2.5 7.0 %copy.27 = bf16[1152,2,1536]{2,0,1:T(8,128)(2,1)} copy(bf16[1152,2,1536]{2,1,0:T(2,128)(2,1)} %param.17) | data formatting | bytes 14155776 | tf_op args[7]
  9.6 0.0 copy-done.2
  9.6 0.0 copy-start.3
  9.6 7.7 %convolution_reduce_fusion = f32[6912]{0:T(1024)S(1)} fusion(bf16[1152,6912]{1,0:T(8,128)(2,1)} %param.13, bf16[1,1152]{1,0:T(2,128)(2,1)S(1)} %copy-done.2), kind=kOutput, calls=%fused_computation.3 | convolution fusion | flops 15932160 | bytes 15955200 | tf_op jit(solution)/shard_map/dot_general | solution.py:712
  17.4 0.0 copy-done.3
  17.4 0.6 reshape.202.mod
  18.0 0.3 fusion.8
  18.3 0.1 broadcast_multiply_fusion.1
  18.4 1.3 fusion.1
  19.6 0.8 broadcast_in_dim.4.valid
  20.5 189.2 %shard_map.169 = (bf16[256,1152]{1,0:T(8,128)(2,1)}, f32[256,1152]{1,0:T(8,128)}, f32[6,1152]{1,0:T(8,128)}, f32[72,7040]{1,0:T(8,128)}) custom-call(bf16[256,1152]{1,0:T(8,128)(2,1)} %tok.1, bf16[256,1152]{1,0:T(8,128)(2,1)} %cot.1, f32[6,1152]{1,0:T(8,128)} %reshape.202.mod, f32[2,72,256]{2,1,0:T(8,128)} %get-tuple-element.40.cos_t, ...), custom_call_target="tpu_custom_call" | custom-call | tf_op jit(solution)/shard_map/pallas_call | solution.py:634
  209.7 0.8 convert_element_type.54
  210.5 0.1 convert_element_type.56
  210.6 0.1 pad.6.clone
  210.7 0.7 reshape.204
  211.4 3.7 %all-to-all-start = ((bf16[32,11,128]{2,1,0:T(8,128)(2,1)}), bf16[32,11,128]{2,1,0:T(8,128)(2,1)S(1)}, u32[]{:S(2)}, u32[]{:S(2)}) async-start(bf16[32,11,128]{2,1,0:T(8,128)(2,1)} %reshape.204), calls=%async_computation | async-start | bytes 262144 | tf_op jit(solution)/shard_map/all_to_all | solution.py:749
  215.1 1.1 slice.28
  216.2 1.2 slice.30
  217.4 1.8 slice_bitcast_fusion
  219.2 0.8 convert_bitcast_fusion
  220.0 0.3 reshape.206
  220.3 0.8 copy.22
  221.1 1.7 reshape.207
  222.8 0.0 copy-start.1
  222.8 0.0 copy-start
  222.8 10.5 %fusion = f32[1,1152]{1,0:T(1,128)} fusion(bf16[6912,1]{0,1:T(2,128)(2,1)S(1)} %bitcast.30, bf16[1152,6912]{1,0:T(8,128)(2,1)} %param.13, bf16[1,1152]{1,0:T(2,128)(2,1)S(1)} %copy-done.2), kind=kOutput, calls=%fused_computation.2 | convolution fusion | flops 15935616 | bytes 15945984 | tf_op jit(solution)/shard_map/dot_general | solution.py:22
  233.3 1.6 slice_bitcast_fusion.1
  234.9 0.0 all-to-all-done
  234.9 1.3 fusion.3
  236.2 0.6 convert_reduce_fusion
  236.8 0.0 copy-done.1
  236.8 0.8 copy.31
  237.6 0.0 copy-done
  237.6 1.0 copy.32
  (8 shorter events, 0.1 us)
Async XLA Ops:
  2.5 7.1 %copy-start.2 = (bf16[1,1152]{1,0:T(2,128)(2,1)S(1)}, bf16[1,1152]{1,0:T(2,128)(2,1)}, u32[]{:S(2)}) copy-start(bf16[1,1152]{1,0:T(2,128)(2,1)} %param.11) | copy-start | bytes 6916
  9.6 7.7 %copy-start.3 = (bf16[6912]{0:T(1024)(128)(2,1)S(1)}, bf16[6912]{0:T(1024)(128)(2,1)}, u32[]{:S(2)}) copy-start(bf16[6912]{0:T(1024)(128)(2,1)} %param.14) | copy-start | bytes 41476
  211.4 23.5 %all-to-all-start = ((bf16[32,11,128]{2,1,0:T(8,128)(2,1)}), bf16[32,11,128]{2,1,0:T(8,128)(2,1)S(1)}, u32[]{:S(2)}, u32[]{:S(2)}) async-start(bf16[32,11,128]{2,1,0:T(8,128)(2,1)} %reshape.204), calls=%async_computation | async-start | bytes 262144 | tf_op jit(solution)/shard_map/all_to_all | solution.py:749
  222.8 14.0 %copy-start.1 = (bf16[256,1152]{1,0:T(8,128)(2,1)S(1)}, bf16[256,1152]{1,0:T(8,128)(2,1)}, u32[]{:S(2)}) copy-start(bf16[256,1152]{1,0:T(8,128)(2,1)} %get-tuple-element.54) | copy-start | bytes 1769476
  222.8 14.8 %copy-start = (f32[256,1152]{1,0:T(8,128)S(1)}, f32[256,1152]{1,0:T(8,128)}, u32[]{:S(2)}) copy-start(f32[256,1152]{1,0:T(8,128)} %get-tuple-element.55) | copy-start | bytes 3538948
where the time goes:
time: 239 us
  Pallas kernels  189 us (79%)
  local copies, waits for them, and re-layouts  20.5 us (9%)
  matrix products  19.5 us (8%)
  other arithmetic  4.97 us (2%)
  starting transfers between devices  3.69 us (2%)
    pallas_call x1, Pallas kernels, run_block(): pl.pallas_call(functools.partial(block_kernel, plan), out_shape=(jax.Shap...  189 us
    dot_general x2, matrix products, dot(): lax.dot_general(left, right, (((left_dim,), (right_dim,)), ((), ())), pre...  11.8 us
    unnamed x14, local copies, waits for them, and re-layouts  9.78 us
    dot_general x1, matrix products, body(): jnp.dot(silu_cond, w_ada, preferred_element_type=F32) + b_ada.astype(F32)  7.72 us
  transfers between devices with their start and end apart: 1, of which 0 were waited for; matrix products, arithmetic and copies ran while one was open for 8% of the time, Pallas kernels for 0%

commit v1 on v0

--- a/solution.py
+++ b/solution.py
@@ -49,12 +49,13 @@
 
 
 def block_kernel(
-    plan, tok, cot, mod, cos_t, sin_t, valid,
-    wqkv_hbm, wout_hbm, wgu_hbm, wdown_hbm,
-    out, dtok, dmod, *rest,
+    plan, tok, cot, cond, grid, bias,
+    wada_hbm, wqkv_hbm, wout_hbm, wgu_hbm, wdown_hbm,
+    out, dtok, *rest,
 ):
     results, rest = rest[: plan["results"]], rest[plan["results"] :]
     (
+        mod, silu_two, cos_t, sin_t, raw,
         wqkv, wout, wg, wu, wdown,
         h1, h2, dml, dat,
         q_s, k_s, v_s, p_s, qkv_f, a_f, a_t,
@@ -62,7 +63,7 @@
         attn, dx1, own,
         send_a, send_c, recv_a, recv_b, recv_c,
         flip, sums,
-        wsem, ssem, rsem, *extra,
+        wsem, asem, ssem, rsem, *extra,
     ) = rest
     width = tok.shape[1]
     heads = q_s.shape[0] // 2
@@ -75,12 +76,41 @@
     loads = [
         pltpu.make_async_copy(src, dst, wsem.at[i])
         for i, (src, dst) in enumerate(
-            (
-                (wqkv_hbm, wqkv), (wout_hbm, wout), (wgu_hbm.at[0], wg), (wgu_hbm.at[1], wu),
-                (wdown_hbm, wdown),
-            )
+            ((wqkv_hbm, wqkv), (wout_hbm, wout), (wdown_hbm, wdown))
         )
     ]
+    half_rows = width // 2
+    slots = [
+        ref.at[pl.ds(n * half_rows, half_rows), pl.ds(0, width)] for ref in (wg, wu) for n in range(2)
+    ]
+
+    class Stream:
+        def __init__(self, blocks, slots):
+            self.chunks = [(b, h) for b in blocks for h in range(2)]
+            self.slots = slots
+            self.copies = []
+            self.at = 0
+
+        def fill(self, most):
+            while len(self.copies) < min(most, len(self.chunks), self.at + len(self.slots)):
+                n = len(self.copies)
+                b, h = self.chunks[n]
+                copy = pltpu.make_async_copy(
+                    wada_hbm.at[pl.ds(h * half_rows, half_rows), pl.ds(b * width, width)],
+                    self.slots[n % len(self.slots)], asem.at[n % len(self.slots)],
+                )
+                copy.start()
+                self.copies.append(copy)
+
+        def take(self):
+            n = self.at
+            self.copies[n].wait()
+            b, h = self.chunks[n]
+            self.at += 1
+            return b, h, self.slots[n % len(self.slots)]
+
+    stream = Stream((0, 1, 5, 2, 3, 4), slots)
+    stream.fill(4)
     for load in loads:
         load.start()
 
@@ -140,20 +170,57 @@
             if copies is not None:
                 copies[c].start()
 
-    shift_one, scale_one, gate_one = mod[0:1], mod[1:2], mod[2:3]
-    shift_two, scale_two, gate_two = mod[3:4], mod[4:5], mod[5:6]
+    cond_f = cond[...].astype(F32)
+    cond_sig = jax.nn.sigmoid(cond_f)
+    silu = (cond_f * cond_sig).astype(BF16)
+    silu_rows = jnp.broadcast_to(silu.astype(F32), (16, width))
+    for h in range(2):
+        silu_two[h] = silu_rows[:, h * half_rows : (h + 1) * half_rows].astype(BF16)
+
+    def modulate(count):
+        for _ in range(count):
+            row = None
+            for _ in range(2):
+                b, h, slot = stream.take()
+                part = dot(silu_two[h], slot[...], 1, 0)[0:1]
+                row = part if row is None else row + part
+                stream.fill(99)
+            mod[b : b + 1, :] = row + bias[b : b + 1, :].astype(F32)
+
+    modulate(2)
+    shift_one, scale_one = mod[0:1], mod[1:2]
 
     def first_norm(rows):
         norm, _ = normed(tok[rows, :].astype(F32))
         h1[0, rows, :] = (norm * (1.0 + scale_one) + shift_one).astype(BF16)
 
     rows_loop(first_norm, go_h1)
+    modulate(1)
+    gate_two = mod[5:6]
 
     def mlp_grad(rows):
         dml[0, rows, :] = (gate_two * cot[rows, :].astype(F32)).astype(BF16)
 
     rows_loop(mlp_grad, go_dml)
     sums[...] = jnp.zeros_like(sums)
+
+    quarter = HD // 4
+    limits = []
+    for image in range(2):
+        at = side if image == 0 else 1 - side
+        tall, wide = grid[at, 0], grid[at, 1]
+        limits.append(tall * wide)
+        spot = lax.broadcasted_iota(jnp.int32, (1, LEN), 1).astype(F32)
+        wide_f = jnp.full((1, LEN), wide, jnp.int32).astype(F32)
+        row_at = jnp.floor((spot + 0.5) / wide_f)
+        col_at = spot - row_at * wide_f
+        step = lax.broadcasted_iota(jnp.int32, (quarter, LEN), 0).astype(F32)
+        frequency = jnp.exp(step * (-9.210340371976184 / quarter))
+        both = jnp.concatenate([row_at * frequency, col_at * frequency], axis=0)
+        for table, turn in ((cos_t, jnp.cos), (sin_t, jnp.sin)):
+            seen = turn(both)
+            first, second = seen[:quarter], seen[quarter:]
+            table[image] = jnp.concatenate([first, first, second, second], axis=0)
 
     def heads_forward(image):
         for part in range(3):
@@ -161,7 +228,7 @@
                 wqkv[part * head_cols : (part + 1) * head_cols, :], h1[image], 1, 1
             )
         cosine, sine = cos_t[image], sin_t[image]
-        ok = valid[image][:, :1] > 0.0
+        ok = lax.broadcasted_iota(jnp.int32, (LEN, LEN), 0) < limits[image]
 
         def head(h, carry):
             at = image * heads + h
@@ -196,12 +263,42 @@
 
     loads[0].wait()
     heads_forward(0)
+    modulate(3)
+    gate_one, shift_two, scale_two = mod[2:3], mod[3:4], mod[4:5]
     for copy in go_h1:
         copy.wait_recv()
     heads_forward(1)
     loads[1].wait()
     strips_of(lambda cols: dot(a_t[1], wout[:, cols], 0, 0), send_a, go_a)
     strips_of(lambda cols: dot(a_t[0], wout[:, cols], 0, 0), keep=own)
+
+    depth = raw.shape[1]
+
+    def fetch(n, slot):
+        return pltpu.make_async_copy(
+            wgu_hbm.at[pl.ds(pl.multiple_of(n * depth, depth), depth)], raw.at[slot], wsem.at[3 + slot]
+        )
+
+    fetch(0, 0).start()
+    r = lax.broadcasted_iota(jnp.int32, (2 * depth, 2 * depth), 0)
+    c = lax.broadcasted_iota(jnp.int32, (2 * depth, 2 * depth), 1)
+    sorter = jnp.where(c == jnp.where(r < depth, 2 * r, 2 * (r - depth) + 1), 1.0, 0.0).astype(BF16)
+
+    def apart(n, carry):
+        slot = lax.rem(n, 2)
+
+        @pl.when(n + 1 < width // depth)
+        def _():
+            fetch(n + 1, 1 - slot).start()
+
+        fetch(n, slot).wait()
+        parted = dot(sorter, raw[slot].reshape(2 * depth, inner), 1, 0).astype(BF16)
+        rows = pl.ds(pl.multiple_of(n * depth, depth), depth)
+        wg[rows, :] = parted[:depth]
+        wu[rows, :] = parted[depth:]
+        return carry
+
+    lax.fori_loop(0, width // depth, apart, 0)
     for copy in go_a:
         copy.wait_recv()
 
@@ -214,8 +311,7 @@
 
     rows_loop(second_norm, go_h2)
 
-    for load in loads[2:]:
-        load.wait()
+    loads[2].wait()
 
     def feed_forward(image):
         def tile(j, carry):
@@ -268,7 +364,13 @@
                 )
 
     if plan["fused"]:
-        (give_one, land0, final, gsend, grecv, osem, credit, *spots) = extra
+        (
+            give_one, land0, final, gsend, grecv, osem, credit, packs, came, dflat, dcond, psem,
+            *spots,
+        ) = extra
+        _, ada_out, cond_out, bias_out = results
+        dflat[...] = jnp.zeros_like(dflat)
+        dcond[...] = jnp.zeros_like(dcond)
         many = len(plan["pieces"])
         land1, land2, land3, held3 = (spots[n * many : (n + 1) * many] for n in range(4))
         half = width // 2
@@ -400,6 +502,80 @@
             "out", y_first, head_cols, v_pad, third[2], 0, results[0], 3 * inner + qk_cols + v_pad
         )
 
+        tail = Stream(
+            (3, 4, 2, 5, 0, 1), [wdown.at[pl.ds(n * half, half)] for n in range(2)] + [wout]
+        )
+        devices = plan["devices"]
+        side_count = plan["sides"]
+        mine = me * side_count + side
+        own_cols = plan["own_cols"]
+
+        def condition_back(blocks):
+            for block in blocks:
+                row = jnp.sum(sums[block], axis=0, keepdims=True)
+                dflat[0:1, block * width : (block + 1) * width] = row
+                rows = jnp.broadcast_to(row, (16, width)).astype(BF16)
+                for _ in range(2):
+                    b, h, slot = tail.take()
+                    dcond[h : h + 1, :] += dot(rows, slot[...], 1, 1)[0:1]
+                    tail.fill(99)
+
+        def share_out():
+            lanes = lax.broadcasted_iota(jnp.int32, (16, 128), 0)
+            base = jnp.zeros((16, 128), F32)
+            silu_f = silu.astype(F32)
+            for n in range(width // 128):
+                base = jnp.where(lanes == n, silu_f[:, n * 128 : (n + 1) * 128], base)
+            row_a = width // 128
+            for n in range(devices):
+                first = dflat[0:1, n * own_cols : n * own_cols + 128]
+                rest = own_cols - 128
+                second = dflat[0:1, n * own_cols + 128 : n * own_cols + 256]
+                packet = jnp.where(lanes == row_a, first, base)
+                packet = jnp.where(lanes == row_a + 1, second, packet)
+                packs[n] = packet.astype(BF16)
+
+            def one(n, carry):
+                other = lax.rem(mine + n, devices)
+                pltpu.make_async_remote_copy(
+                    src_ref=packs.at[other], dst_ref=came.at[mine], send_sem=psem.at[0],
+                    recv_sem=psem.at[1],
+                    device_id={
+                        "dp": lax.div(other, side_count), "tensor": lax.rem(other, side_count)
+                    },
+                    device_id_type=MESH,
+                ).start()
+                return carry
+
+            lax.fori_loop(1, devices, one, 0)
+            came[mine] = packs[mine]
+
+        def take_in():
+            every = pl.ds(0, devices - 1)
+            whole = pltpu.make_async_remote_copy(
+                src_ref=packs.at[every], dst_ref=came.at[every], send_sem=psem.at[0],
+                recv_sem=psem.at[1], device_id=mate, device_id_type=MESH,
+            )
+            whole.wait_send()
+            whole.wait_recv()
+            seen = came[...].astype(F32)
+            row_a = width // 128
+            silu_all = jnp.concatenate([seen[:, n, :] for n in range(row_a)], axis=1).astype(BF16)
+            columns = jnp.concatenate([seen[:, row_a, :], seen[:, row_a + 1, :]], axis=1)
+            bias_out[...] = jnp.broadcast_to(jnp.sum(columns, axis=0, keepdims=True), bias_out.shape)
+            value = dot(silu_all, columns.astype(BF16), 0, 0)
+            for n in range(-(-width // LEN)):
+                size = min(LEN, width - n * LEN)
+                p_s[n, 0:size, :] = value[n * LEN : n * LEN + size]
+                copy = pltpu.make_async_copy(
+                    p_s.at[n, pl.ds(0, size)], ada_out.at[pl.ds(n * LEN, size)], asem.at[n]
+                )
+                copy.start()
+                copy.wait()
+            slope = cond_sig * (1.0 + cond_f * (1.0 - cond_sig))
+            whole_row = jnp.concatenate([dcond[0:1, :], dcond[1:2, :]], axis=1)
+            cond_out[...] = whole_row * slope
+
     def lane_right(array):
         def right(start, size):
             if not isinstance(start, int):
@@ -501,6 +677,18 @@
         dqkv[image] = qkv_f[...].astype(BF16)
 
     heads_back(0)
+    strips_of(mlp_strip(0), keep=own)
+    for copy in go_c:
+        copy.wait_recv()
+
+    def finish(rows):
+        branch = own[rows, :] + recv_c[rows, :].astype(F32)
+        out[rows, :] = (
+            tok[rows, :].astype(F32) + gate_one * attn[rows, :] + gate_two * branch
+        ).astype(BF16)
+        sums[5] += fold(cot[rows, :].astype(F32) * branch)
+
+    rows_loop(finish)
     if plan["fused"]:
         p_up.add(0)
     for copy in go_dat:
@@ -532,6 +720,8 @@
         p_down.add(1)
         p_up.add(1)
         p_out.add(0)
+        tail.fill(99)
+        condition_back((3, 4, 2, 5))
     else:
         plain_grad_in(h1, row_right(dqkv, 0), 3 * head_cols, results[3])
         plain_grad_in(dat, row_right(a_t, 0), head_cols, results[4])
@@ -548,24 +738,16 @@
 
     rows_loop(first_back)
 
-    strips_of(mlp_strip(0), keep=own)
-    for copy in go_c:
-        copy.wait_recv()
-
-    def finish(rows):
-        branch = own[rows, :] + recv_c[rows, :].astype(F32)
-        out[rows, :] = (
-            tok[rows, :].astype(F32) + gate_one * attn[rows, :] + gate_two * branch
-        ).astype(BF16)
-        sums[5] += fold(cot[rows, :].astype(F32) * branch)
-
-    rows_loop(finish)
-    for n in range(6):
-        dmod[n : n + 1, :] = jnp.sum(sums[n], axis=0, keepdims=True)
+    if plan["fused"]:
+        condition_back((0, 1))
+    else:
+        for n in range(6):
+            results[5][n : n + 1, :] = jnp.sum(sums[n], axis=0, keepdims=True)
     if plan["fused"]:
         p_down.add(2)
         p_gate.add(1)
         p_down.add(3)
+        share_out()
         p_up.add(2)
         p_qk.add(1)
         p_gate.add(2)
@@ -579,6 +761,7 @@
         p_out.add(2)
         p_v.add(3)
         p_out.add(3)
+        take_in()
         state["final"].wait()
         pl.semaphore_wait(credit, 1)
         for piece in (p_gate, p_up, p_qk, p_v, p_out, p_down):
@@ -589,23 +772,32 @@
         copy.wait_send()
 
 
-def run_block(tok, cot, mod, cos_t, sin_t, valid, wqkv, wout, wgu, wdown):
+def run_block(tok, cot, cond, grid, bias, wada, wqkv, wout, wgu, wdown):
     width = tok.shape[1]
     head_cols = wout.shape[0]
     heads = head_cols // HD
     inner = wdown.shape[0]
     strips = width // STRIP
     count = lax.axis_size("dp")
+    sides = lax.axis_size("tensor")
+    devices = count * sides
+    own_cols = 6 * width // devices
     vmem = pl.BlockSpec(memory_space=pltpu.VMEM)
     hbm = pl.BlockSpec(memory_space=pl.ANY)
     V = pltpu.VMEM
     D = pltpu.SemaphoreType.DMA
     copies = 8 + 4 * strips
-    fused = count == 16 and width % (8 * count) == 0
+    fused = count == 16 and width % (8 * count) == 0 and 128 < own_cols <= 256
     names = ["down", "gate", "up", "qk", "v", "out"]
     pad = -(-head_cols // 128) * 128
     if fused:
-        results = [jax.ShapeDtypeStruct((width // count, 3 * inner + 2 * head_cols + 2 * pad), F32)]
+        results = [
+            jax.ShapeDtypeStruct((width // count, 3 * inner + 2 * head_cols + 2 * pad), F32),
+            jax.ShapeDtypeStruct((width, 256), F32),
+            jax.ShapeDtypeStruct((1, width), F32),
+            jax.ShapeDtypeStruct((8, 256), F32),
+        ]
+        result_specs = [hbm, hbm, vmem, vmem]
         chunk = width // count
         widths = [inner, inner, inner, 2 * head_cols, pad, pad]
         extra = [
@@ -616,6 +808,11 @@
             D((len(names), 4)),
             D(()),
             pltpu.SemaphoreType.REGULAR,
+            V((devices, 16, 128), BF16),
+            V((devices, 16, 128), BF16),
+            V((8, 6 * width + 128), F32),
+            V((8, width // 2), F32),
+            D((2,)),
             *[V((width // 4, w), BF16) for w in widths],
             *[V((width // 8, w), BF16) for w in widths],
             *[V((1, chunk, w), BF16) for w in widths],
@@ -625,10 +822,13 @@
     else:
         wide = [inner, inner, inner, 3 * head_cols, head_cols]
         results = [jax.ShapeDtypeStruct((width, -(-w // TILE) * TILE), BF16) for w in wide]
+        results += [jax.ShapeDtypeStruct((6, width), F32)]
+        result_specs = [hbm] * 5 + [vmem]
         extra = [V((2, width, TILE), BF16), D((2,))]
         strides = []
     plan = {
         "fused": fused, "results": len(results), "count": count, "pieces": names,
+        "devices": devices, "sides": sides, "own_cols": own_cols,
         "strides": strides, "orders": ((1, 2, 4, 8), (1, 4, 2, 8)),
     }
     return pl.pallas_call(
@@ -636,14 +836,15 @@
         out_shape=(
             jax.ShapeDtypeStruct((LEN, width), BF16),
             jax.ShapeDtypeStruct((LEN, width), F32),
-            jax.ShapeDtypeStruct((6, width), F32),
             *results,
         ),
-        in_specs=[vmem] * 6 + [hbm] * 4,
-        out_specs=[vmem] * 3 + [hbm] * len(results),
+        in_specs=[vmem] * 3 + [pl.BlockSpec(memory_space=pltpu.SMEM), vmem] + [hbm] * 5,
+        out_specs=[vmem] * 2 + result_specs,
         scratch_shapes=[
-            V(wqkv.shape, BF16), V(wout.shape, BF16), V(wgu.shape[1:], BF16),
-            V(wgu.shape[1:], BF16), V(wdown.shape, BF16),
+            V((8, width), F32), V((2, 16, width // 2), BF16), V((2, HD, LEN), F32),
+            V((2, HD, LEN), F32), V((2, 32, 2, inner), BF16),
+                        V(wqkv.shape, BF16), V(wout.shape, BF16), V((width, inner), BF16),
+            V((width, inner), BF16), V(wdown.shape, BF16),
             *[V((2, LEN, width), BF16)] * 4,
             *[V((2 * heads, HD, LEN), BF16)] * 3,
             V((2 * heads, LEN, LEN), F32),
@@ -657,6 +858,7 @@
             V((width, 2 * LEN), BF16),
             V((6, 8, width), F32),
             D((5,)),
+            D((8,)),
             D((copies,)),
             D((copies,)),
             *extra,
@@ -664,22 +866,7 @@
         compiler_params=pltpu.CompilerParams(
             collective_id=0, has_side_effects=True, vmem_limit_bytes=62 * 1024 * 1024
         ),
-    )(tok, cot, mod, cos_t, sin_t, valid, wqkv, wout, wgu, wdown)
-
-
-def rope_tables(grid_shape):
-    position = jnp.arange(LEN, dtype=jnp.int32)[None, :]
-    widths = grid_shape[:, 1:2]
-    rows_at = position // widths
-    cols_at = position % widths
-    key_valid = position < grid_shape[:, 0:1] * widths
-    quarter = HD // 4
-    frequency = 10000.0 ** (-jnp.arange(quarter, dtype=F32) / quarter)
-    row_angle = rows_at.astype(F32)[:, None, :] * frequency[:, None]
-    col_angle = cols_at.astype(F32)[:, None, :] * frequency[:, None]
-    angles = jnp.concatenate([row_angle, row_angle, col_angle, col_angle], axis=1)
-    valid = jnp.broadcast_to(key_valid.astype(F32)[:, :, None], (*key_valid.shape, 128))
-    return jnp.cos(angles), jnp.sin(angles), valid
+    )(tok, cot, cond, grid, bias, wada, wqkv, wout, wgu, wdown)
 
 
 def sum_over_images(partial):
@@ -706,21 +893,17 @@
     width = tokens.shape[1]
     inner = w_down.shape[0]
     head_cols = w_out.shape[0]
-    cond = condition.astype(F32)
-    cond_sigmoid = jax.nn.sigmoid(cond)
-    silu_cond = (cond * cond_sigmoid).astype(BF16)
-    mod = jnp.dot(silu_cond, w_ada, preferred_element_type=F32) + b_ada.astype(F32)
-    mod = mod.reshape(6, width)
-    mine = lax.axis_index("tensor")
-    grid_shape = jnp.where(mine == 0, grid_shape, grid_shape[::-1])
-    cos_t, sin_t, valid = rope_tables(grid_shape)
     wqkv = w_qkv.transpose(1, 2, 0).reshape(3 * head_cols, width)
-    layer_out, d_tokens, d_mod, *grads = run_block(
-        tokens, cotangent, mod, cos_t, sin_t, valid, wqkv, w_out,
-        w_gate_up.transpose(1, 0, 2), w_down,
+    layer_out, d_tokens, *grads = run_block(
+        tokens, cotangent, condition, grid_shape, b_ada.reshape(6, width), w_ada, wqkv, w_out,
+        w_gate_up, w_down,
     )
-    if len(grads) == 1:
-        whole = grads[0]
+    devices_all = lax.axis_size("dp") * lax.axis_size("tensor")
+    own_cols = 6 * width // devices_all
+    if len(grads) == 4:
+        whole, ada, d_condition, bias_rows = grads
+        weight_part = ada[:, :own_cols]
+        bias_part = bias_rows[0, :own_cols]
         pad = -(-head_cols // 128) * 128
         grad_down = whole[:, :inner].T
         grad_gate_up = whole[:, inner : 3 * inner].reshape(-1, 2, inner)
@@ -732,27 +915,28 @@
         grad_gate_up = jnp.stack([sum_over_images(grads[1]), sum_over_images(grads[2])], axis=1)
         grad_qkv = sum_over_images(grads[3][:, : 3 * head_cols]).reshape(-1, 3, head_cols)
         grad_out = sum_over_images(grads[4][:, :head_cols]).T
-    d_mod = d_mod.reshape(1, 6 * width).astype(BF16)
-    d_condition = (
-        dot(d_mod, w_ada, 1, 1) * cond_sigmoid * (1.0 + cond * (1.0 - cond_sigmoid))
-    )
-    devices_all = lax.axis_size("dp") * lax.axis_size("tensor")
-    own_cols = 6 * width // devices_all
-    packed = jnp.concatenate(
-        [
-            d_mod.reshape(devices_all, own_cols),
-            jnp.broadcast_to(silu_cond, (devices_all, width)),
-        ],
-        axis=1,
-    )
-    packed = jnp.pad(packed, ((0, 0), (0, -packed.shape[1] % 128)))
-    packed = lax.all_to_all(
-        packed.reshape(devices_all, -1, 128), ("dp", "tensor"), 0, 0, tiled=True
-    ).reshape(devices_all, -1)
-    columns = packed[:, :own_cols]
-    silu_rows = packed[:, own_cols : own_cols + width]
-    weight_part = dot(silu_rows, columns, 0, 0)
-    bias_part = jnp.sum(columns.astype(F32), axis=0)
+        cond = condition.astype(F32)
+        cond_sigmoid = jax.nn.sigmoid(cond)
+        silu_cond = (cond * cond_sigmoid).astype(BF16)
+        d_mod = grads[5].reshape(1, 6 * width).astype(BF16)
+        d_condition = (
+            dot(d_mod, w_ada, 1, 1) * cond_sigmoid * (1.0 + cond * (1.0 - cond_sigmoid))
+        )
+        packed = jnp.concatenate(
+            [
+                d_mod.reshape(devices_all, own_cols),
+                jnp.broadcast_to(silu_cond, (devices_all, width)),
+            ],
+            axis=1,
+        )
+        packed = jnp.pad(packed, ((0, 0), (0, -packed.shape[1] % 128)))
+        packed = lax.all_to_all(
+            packed.reshape(devices_all, -1, 128), ("dp", "tensor"), 0, 0, tiled=True
+        ).reshape(devices_all, -1)
+        columns = packed[:, :own_cols]
+        silu_rows = packed[:, own_cols : own_cols + width]
+        weight_part = dot(silu_rows, columns, 0, 0)
+        bias_part = jnp.sum(columns.astype(F32), axis=0)
     return (
         layer_out, d_tokens, d_condition, weight_part, bias_part,
         grad_qkv, grad_out, grad_gate_up, grad_down,

time: 239 us -> 217 us (0.908); the launches traced: 239 us -> 214 us
  matrix products: 19.5 us -> 0 us
  Pallas kernels: 189 us -> 199 us
  local copies, waits for them, and re-layouts: 20.5 us -> 14.8 us
  other arithmetic: 4.97 us -> 0 us
  starting transfers between devices: 3.69 us -> 0 us
    dot_general x3 -> x0, matrix products: 19.5 us -> none  [the longest x2 11.8 us: dot(): lax.dot_general(left, right, (((left_dim,), (right_dim,)), ((), ())), pre...]
    pallas_call x1, Pallas kernels: 189 us -> 199 us  [run_block(): pl.pallas_call(functools.partial(block_kernel, plan), out_shape=(jax.Shap...]
    unnamed x14 -> x13, local copies, waits for them, and re-layouts: 9.78 us -> 4.58 us
    all_to_all x1 -> x0, starting transfers between devices: 3.69 us -> none  [body(): lax.all_to_all(packed.reshape(devices_all, -1, 128), ('dp', 'tensor'), 0,...]
  transfers between devices with their start and end apart: 1 -> 0, of which waited for: 0 -> 0; matrix products, arithmetic and copies ran while one was open for 8% -> 0% of each run, Pallas kernels for 0% -> 0%
where the time goes in v1:
time: 217 us; the launch traced here: 214 us
  Pallas kernels  199 us (92%)
  local copies, waits for them, and re-layouts  14.8 us (7%)
    pallas_call x1, Pallas kernels, run_block(): pl.pallas_call(functools.partial(block_kernel, plan), out_shape=(jax.Shap...  199 us
    unnamed x13, local copies, waits for them, and re-layouts  4.58 us

profile of v1, /device:TPU:0, one launch (start us, length us, event | category | flops | bytes accessed | tf_op | source)
XLA Modules:
  0.0 214.1 jit_solution(4415286024674336291)
XLA Ops:
  0.6 1.4 reshape.30.bias
  2.0 198.5 %shard_map.169 = (bf16[256,1152]{1,0:T(8,128)(2,1)}, f32[256,1152]{1,0:T(8,128)}, f32[72,7040]{1,0:T(8,128)}, f32[1152,256]{1,0:T(8,128)}, f32[1,1152]{1,0:T(1,128)}, /*index=5*/f32[8,256]{1,0:T(8,128)}) custom-call(bf16[256,1152]{1,0:T(8,128)(2,1)} %tok.1, bf16[256,1152]{1,0:T(8,128)(2,1)} %cot.1, bf16[1,1152]{1,0:T(2,128)(2,1)} %cond.1, s32[2,2]{1,0:T(2,128)} %grid.1, ...), custom_call_target="tpu_custom_call" | custom-call | tf_op jit(solution)/shard_map/pallas_call | solution.py:834
  200.5 1.3 slice.19
  201.8 1.6 slice_bitcast_fusion.1
  203.4 1.8 slice_bitcast_fusion
  205.2 1.1 slice.20
  206.3 1.2 slice.22
  207.5 0.0 copy-start.1
  207.5 1.7 reshape.33
  209.2 0.3 reshape.32
  209.5 0.0 copy-start
  209.5 0.8 copy.22
  210.3 0.0 copy-done.1
  210.3 0.0 copy-start.2
  210.3 1.3 copy.21
  211.6 0.0 copy-done.2
  211.6 0.0 copy-start.3
  211.6 0.8 copy.26
  212.4 0.0 copy-done
  212.4 1.0 copy.27
  213.5 0.0 copy-done.3
  213.5 0.6 copy.28
Async XLA Ops:
  207.5 2.8 %copy-start.1 = (f32[1152,256]{1,0:T(8,128)S(1)}, f32[1152,256]{1,0:T(8,128)}, u32[]{:S(2)}) copy-start(f32[1152,256]{1,0:T(8,128)} %get-tuple-element.18) | copy-start | bytes 3538948
  209.5 3.0 %copy-start = (f32[256,1152]{1,0:T(8,128)S(1)}, f32[256,1152]{1,0:T(8,128)}, u32[]{:S(2)}) copy-start(f32[256,1152]{1,0:T(8,128)} %get-tuple-element.49) | copy-start | bytes 3538948
  210.3 1.3 copy-start.2
  211.6 1.8 copy-start.3

commit v2 on v1

--- a/solution.py
+++ b/solution.py
@@ -61,7 +61,7 @@
         q_s, k_s, v_s, p_s, qkv_f, a_f, a_t,
         hid, dgate, dup, dqkv,
         attn, dx1, own,
-        send_a, send_c, recv_a, recv_b, recv_c,
+        send_a, send_c, recv_a, recv_c, row_out, row_in,
         flip, sums,
         wsem, asem, ssem, rsem, *extra,
     ) = rest
@@ -126,7 +126,6 @@
     friends = [mate] + [partner(s) for s in plan["strides"]]
     for friend in friends:
         pl.semaphore_signal(barrier, inc=1, device_id=friend, device_id_type=MESH)
-    pl.semaphore_wait(barrier, len(friends))
 
     def give(src, dst, slot):
         return pltpu.make_async_remote_copy(
@@ -151,11 +150,16 @@
             for c in range(strips)
         ]
 
-    go_h1, go_dml, go_h2, go_dat = (gather(b, 2 * i) for i, b in enumerate((h1, dml, h2, dat)))
+    go_h1, go_h2, go_dat = (gather(b, 2 * i) for i, b in enumerate((h1, h2, dat)))
+    go_cot = [
+        give(cot.at[pl.ds(c * (LEN // 2), LEN // 2)], dml.at[1, pl.ds(c * (LEN // 2), LEN // 2)], 6 + c)
+        for c in range(2)
+    ]
+    go_row = give(row_out, row_in, 8 + 4 * (width // STRIP))
     go_a, go_b, go_c, go_d = (
         scatter(s, r, 8 + strips * i)
         for i, (s, r) in enumerate(
-            ((send_a, recv_a), (send_a, recv_b), (send_c, recv_c), (send_a, recv_a))
+            ((send_a, recv_a), (send_a, recv_a), (send_c, recv_c), (send_a, recv_a))
         )
     )
 
@@ -177,6 +181,12 @@
     for h in range(2):
         silu_two[h] = silu_rows[:, h * half_rows : (h + 1) * half_rows].astype(BF16)
 
+    bias_f = bias[...].astype(F32)
+    tiles = width // bias.shape[1]
+
+    def bias_row(b):
+        return jnp.concatenate([bias_f[b * tiles + n : b * tiles + n + 1] for n in range(tiles)], axis=1)
+
     def modulate(count):
         for _ in range(count):
             row = None
@@ -185,23 +195,27 @@
                 part = dot(silu_two[h], slot[...], 1, 0)[0:1]
                 row = part if row is None else row + part
                 stream.fill(99)
-            mod[b : b + 1, :] = row + bias[b : b + 1, :].astype(F32)
-
+            mod[b : b + 1, :] = row + bias_row(b)
+
+    def pre_norm(rows):
+        norm, _ = normed(tok[rows, :].astype(F32))
+        dx1[rows, :] = norm
+
+    rows_loop(pre_norm)
+    pl.semaphore_wait(barrier, len(friends))
+    go_cot[0].start()
     modulate(2)
     shift_one, scale_one = mod[0:1], mod[1:2]
 
     def first_norm(rows):
-        norm, _ = normed(tok[rows, :].astype(F32))
-        h1[0, rows, :] = (norm * (1.0 + scale_one) + shift_one).astype(BF16)
+        h1[0, rows, :] = (dx1[rows, :] * (1.0 + scale_one) + shift_one).astype(BF16)
 
     rows_loop(first_norm, go_h1)
     modulate(1)
     gate_two = mod[5:6]
-
-    def mlp_grad(rows):
-        dml[0, rows, :] = (gate_two * cot[rows, :].astype(F32)).astype(BF16)
-
-    rows_loop(mlp_grad, go_dml)
+    row_out[...] = jnp.broadcast_to(gate_two, row_out.shape)
+    go_row.start()
+    go_cot[1].start()
     sums[...] = jnp.zeros_like(sums)
 
     quarter = HD // 4
@@ -222,6 +236,31 @@
             first, second = seen[:quarter], seen[quarter:]
             table[image] = jnp.concatenate([first, first, second, second], axis=0)
 
+    depth = raw.shape[1]
+    ring = raw.shape[0]
+    parts = {"next": 0, "copies": []}
+    r = lax.broadcasted_iota(jnp.int32, (2 * depth, 2 * depth), 0)
+    c = lax.broadcasted_iota(jnp.int32, (2 * depth, 2 * depth), 1)
+    sorter = jnp.where(c == jnp.where(r < depth, 2 * r, 2 * (r - depth) + 1), 1.0, 0.0).astype(BF16)
+
+    def fetch(n):
+        if n < width // depth:
+            copy = pltpu.make_async_copy(
+                wgu_hbm.at[pl.ds(n * depth, depth)], raw.at[n % ring], wsem.at[3 + n % ring]
+            )
+            copy.start()
+            parts["copies"].append(copy)
+
+    def pull_apart(until):
+        while parts["next"] < until:
+            n = parts["next"]
+            parts["copies"][n].wait()
+            parted = dot(sorter, raw[n % ring].reshape(2 * depth, inner), 1, 0).astype(BF16)
+            wg[n * depth : (n + 1) * depth, :] = parted[:depth]
+            wu[n * depth : (n + 1) * depth, :] = parted[depth:]
+            fetch(n + ring)
+            parts["next"] += 1
+
     def heads_forward(image):
         for part in range(3):
             qkv_f[part * head_cols : (part + 1) * head_cols, :] = dot(
@@ -248,7 +287,7 @@
             a_f[rows, :] = dot(value, probs.astype(BF16), 1, 0)
             return carry
 
-        lax.fori_loop(0, heads, head, 0)
+        lax.fori_loop(0, heads, head, 0, unroll=2)
         a_t[image] = a_f[...].astype(BF16)
 
     def strips_of(make, send=None, copies=None, keep=None):
@@ -261,9 +300,12 @@
             else:
                 keep[:, cols] = value
 
+    for n in range(ring):
+        fetch(n)
     loads[0].wait()
     heads_forward(0)
     modulate(3)
+    pull_apart(plan["early"])
     gate_one, shift_two, scale_two = mod[2:3], mod[3:4], mod[4:5]
     for copy in go_h1:
         copy.wait_recv()
@@ -272,33 +314,18 @@
     strips_of(lambda cols: dot(a_t[1], wout[:, cols], 0, 0), send_a, go_a)
     strips_of(lambda cols: dot(a_t[0], wout[:, cols], 0, 0), keep=own)
 
-    depth = raw.shape[1]
-
-    def fetch(n, slot):
-        return pltpu.make_async_copy(
-            wgu_hbm.at[pl.ds(pl.multiple_of(n * depth, depth), depth)], raw.at[slot], wsem.at[3 + slot]
-        )
-
-    fetch(0, 0).start()
-    r = lax.broadcasted_iota(jnp.int32, (2 * depth, 2 * depth), 0)
-    c = lax.broadcasted_iota(jnp.int32, (2 * depth, 2 * depth), 1)
-    sorter = jnp.where(c == jnp.where(r < depth, 2 * r, 2 * (r - depth) + 1), 1.0, 0.0).astype(BF16)
-
-    def apart(n, carry):
-        slot = lax.rem(n, 2)
-
-        @pl.when(n + 1 < width // depth)
-        def _():
-            fetch(n + 1, 1 - slot).start()
-
-        fetch(n, slot).wait()
-        parted = dot(sorter, raw[slot].reshape(2 * depth, inner), 1, 0).astype(BF16)
-        rows = pl.ds(pl.multiple_of(n * depth, depth), depth)
-        wg[rows, :] = parted[:depth]
-        wu[rows, :] = parted[depth:]
-        return carry
-
-    lax.fori_loop(0, width // depth, apart, 0)
+    for copy in go_cot:
+        copy.wait_recv()
+    go_row.wait_recv()
+    gate_mate = row_in[0:1]
+
+    def mlp_grad(rows):
+        dml[0, rows, :] = (gate_two * cot[rows, :].astype(F32)).astype(BF16)
+        dml[1, rows, :] = (gate_mate * dml[1, rows, :].astype(F32)).astype(BF16)
+
+    rows_loop(mlp_grad)
+
+    pull_apart(width // depth)
     for copy in go_a:
         copy.wait_recv()
 
@@ -328,8 +355,6 @@
 
         lax.fori_loop(0, inner // TILE, tile, 0)
 
-    for copy in go_dml:
-        copy.wait_recv()
     feed_forward(0)
     for copy in go_h2:
         copy.wait_recv()
@@ -344,7 +369,6 @@
     for copy in go_a:
         copy.wait_send()
     strips_of(dh2_strip(1), send_a, go_b)
-    strips_of(mlp_strip(1), send_c, go_c)
     strips_of(dh2_strip(0), keep=own)
 
     def turned(left, order):
@@ -365,7 +389,7 @@
 
     if plan["fused"]:
         (
-            give_one, land0, final, gsend, grecv, osem, credit, packs, came, dflat, dcond, psem,
+            give_one, keep_out, land0, final, gsend, grecv, osem, credit, packs, came, dflat, dcond, psem,
             *spots,
         ) = extra
         _, ada_out, cond_out, bias_out = results
@@ -492,15 +516,23 @@
         low, high = wg.at[pl.ds(0, half)], wg.at[pl.ds(half, half)]
         third = [wqkv.at[pl.ds(n * half, half)] for n in range(3)]
         p_down = Piece("down", y_first, inner, inner, low, 0, results[0], 0)
-        p_gate = Piece("gate", y_first, inner, inner, high, 0, results[0], inner)
-        p_up = Piece("up", z_first, inner, inner, wu.at[pl.ds(0, half)], 0, results[0], 2 * inner)
-        qk_cols = 2 * head_cols
-        v_pad = -(-head_cols // 128) * 128
-        p_qk = Piece("qk", y_first, qk_cols, qk_cols, third[0], 0, results[0], 3 * inner)
-        p_v = Piece("v", y_first, head_cols, v_pad, third[1], 0, results[0], 3 * inner + qk_cols)
-        p_out = Piece(
-            "out", y_first, head_cols, v_pad, third[2], 0, results[0], 3 * inner + qk_cols + v_pad
-        )
+        p_gate = Piece("gate", z_first, inner, inner, high, 0, results[0], inner)
+        p_up = Piece("up", y_first, inner, inner, wu.at[pl.ds(0, half)], 0, results[0], 2 * inner)
+        pad = -(-head_cols // 128) * 128
+        small = [
+            Piece(
+                name, order, head_cols, pad, place, offset, results[0], 3 * inner + n * pad
+            )
+            for n, (name, order, place, offset) in enumerate(
+                (
+                    ("q", y_first, third[0], 0),
+                    ("k", z_first, third[1], 0),
+                    ("v", y_first, third[2], 0),
+                    ("out", y_first, keep_out, 0),
+                )
+            )
+        ]
+        p_q, p_k, p_v, p_out = small
 
         tail = Stream(
             (3, 4, 2, 5, 0, 1), [wdown.at[pl.ds(n * half, half)] for n in range(2)] + [wout]
@@ -563,15 +595,10 @@
             silu_all = jnp.concatenate([seen[:, n, :] for n in range(row_a)], axis=1).astype(BF16)
             columns = jnp.concatenate([seen[:, row_a, :], seen[:, row_a + 1, :]], axis=1)
             bias_out[...] = jnp.broadcast_to(jnp.sum(columns, axis=0, keepdims=True), bias_out.shape)
-            value = dot(silu_all, columns.astype(BF16), 0, 0)
-            for n in range(-(-width // LEN)):
-                size = min(LEN, width - n * LEN)
-                p_s[n, 0:size, :] = value[n * LEN : n * LEN + size]
-                copy = pltpu.make_async_copy(
-                    p_s.at[n, pl.ds(0, size)], ada_out.at[pl.ds(n * LEN, size)], asem.at[n]
-                )
-                copy.start()
-                copy.wait()
+            own[...] = dot(columns.astype(BF16), silu_all, 0, 0)
+            copy = pltpu.make_async_copy(own.at[pl.ds(0, own_cols)], ada_out, asem.at[0])
+            copy.start()
+            copy.wait()
             slope = cond_sig * (1.0 + cond_f * (1.0 - cond_sig))
             whole_row = jnp.concatenate([dcond[0:1, :], dcond[1:2, :]], axis=1)
             cond_out[...] = whole_row * slope
@@ -616,10 +643,10 @@
         plain_grad(right, columns, target)
 
     if plan["fused"]:
-        turned(dml, y_first)
+        turned(dml, p_down.order)
         p_down.compute(lane_right(hid), 0)
         p_down.go()
-        turned(h2, y_first)
+        turned(h2, p_gate.order)
         p_gate.compute(lane_right(dgate), 1)
         p_down.add(0)
         p_gate.go()
@@ -632,7 +659,7 @@
         copy.wait_recv()
 
     def second_back(rows):
-        grad = own[rows, :] + recv_b[rows, :].astype(F32)
+        grad = own[rows, :] + recv_a[rows, :].astype(F32)
         norm, inverse = normed(tok[rows, :].astype(F32) + gate_one * attn[rows, :])
         middle = cot[rows, :].astype(F32) + norm_back(grad * (1.0 + scale_two), norm, inverse)
         dx1[rows, :] = middle
@@ -643,10 +670,11 @@
 
     rows_loop(second_back, go_dat)
 
+    strips_of(mlp_strip(1), send_c, go_c)
     if plan["fused"]:
         p_gate.add(0)
         p_down.copies[0].wait_send()
-        turned(h2, z_first)
+        turned(h2, p_up.order)
         p_up.compute(lane_right(dup), 0)
         p_up.go()
 
@@ -673,10 +701,63 @@
             qkv_f[pl.ds(pl.multiple_of(2 * head_cols + h * HD, 8), HD), :] = dvalue
             return carry
 
-        lax.fori_loop(0, heads, head, 0)
+        lax.fori_loop(0, heads, head, 0, unroll=2)
         dqkv[image] = qkv_f[...].astype(BF16)
 
     heads_back(0)
+    if plan["fused"]:
+        p_up.add(0)
+    for copy in go_dat:
+        copy.wait_recv()
+    heads_back(1)
+
+    def dh1_strip(image):
+        return lambda cols: dot(dqkv[image], wqkv[:, cols], 0, 0)
+
+    for copy in go_b:
+        copy.wait_send()
+    strips_of(dh1_strip(1), send_a, go_d)
+    strips_of(dh1_strip(0), keep=own)
+
+    if plan["fused"]:
+        p_gate.copies[0].wait_send()
+        p_up.copies[0].wait_send()
+        p_down.add(1)
+        p_gate.add(1)
+        turned(h1, p_q.order)
+        p_q.compute(row_right(dqkv, 0), 0)
+        p_q.go()
+        p_v.compute(row_right(dqkv, 2 * head_cols), 1)
+        p_q.add(0)
+        p_v.go()
+        p_q.copies[0].wait_send()
+        turned(h1, p_k.order)
+        p_k.compute(row_right(dqkv, head_cols), 0)
+        p_v.add(0)
+        p_k.go()
+        p_v.copies[0].wait_send()
+        turned(dat, p_out.order)
+        p_out.compute(row_right(a_t, 0), 1)
+        p_k.add(0)
+        p_out.go()
+        p_down.add(2)
+        p_out.add(0)
+    else:
+        plain_grad_in(h1, row_right(dqkv, 0), 3 * head_cols, results[3])
+        plain_grad_in(dat, row_right(a_t, 0), head_cols, results[4])
+
+    for copy in go_d:
+        copy.wait_recv()
+
+    def first_back(rows):
+        grad = own[rows, :] + recv_a[rows, :].astype(F32)
+        norm, inverse = normed(tok[rows, :].astype(F32))
+        dtok[rows, :] = dx1[rows, :] + norm_back(grad * (1.0 + scale_one), norm, inverse)
+        sums[0] += fold(grad)
+        sums[1] += fold(grad * norm)
+
+    rows_loop(first_back)
+
     strips_of(mlp_strip(0), keep=own)
     for copy in go_c:
         copy.wait_recv()
@@ -690,86 +771,76 @@
 
     rows_loop(finish)
     if plan["fused"]:
-        p_up.add(0)
-    for copy in go_dat:
-        copy.wait_recv()
-    heads_back(1)
-
-    def dh1_strip(image):
-        return lambda cols: dot(dqkv[image], wqkv[:, cols], 0, 0)
-
-    for copy in go_b:
-        copy.wait_send()
-    strips_of(dh1_strip(1), send_a, go_d)
-    strips_of(dh1_strip(0), keep=own)
-
-    if plan["fused"]:
-        p_gate.copies[0].wait_send()
-        p_up.copies[0].wait_send()
-        turned(h1, y_first)
-        p_qk.compute(row_right(dqkv, 0), 0)
-        p_qk.go()
-        p_v.compute(row_right(dqkv, 2 * head_cols), 1)
-        p_qk.add(0)
-        p_v.go()
-        p_qk.copies[0].wait_send()
-        turned(dat, y_first)
-        p_out.compute(row_right(a_t, 0), 0)
-        p_v.add(0)
-        p_out.go()
-        p_down.add(1)
+        tail.fill(99)
         p_up.add(1)
-        p_out.add(0)
-        tail.fill(99)
-        condition_back((3, 4, 2, 5))
-    else:
-        plain_grad_in(h1, row_right(dqkv, 0), 3 * head_cols, results[3])
-        plain_grad_in(dat, row_right(a_t, 0), head_cols, results[4])
-
-    for copy in go_d:
-        copy.wait_recv()
-
-    def first_back(rows):
-        grad = own[rows, :] + recv_a[rows, :].astype(F32)
-        norm, inverse = normed(tok[rows, :].astype(F32))
-        dtok[rows, :] = dx1[rows, :] + norm_back(grad * (1.0 + scale_one), norm, inverse)
-        sums[0] += fold(grad)
-        sums[1] += fold(grad * norm)
-
-    rows_loop(first_back)
-
-    if plan["fused"]:
+        condition_back((3, 4))
+        p_down.add(3)
+        condition_back((2, 5))
+        p_gate.add(2)
         condition_back((0, 1))
+        share_out()
+        p_up.add(2)
+        p_k.add(1)
+        p_q.add(1)
+        p_gate.add(3)
+        p_up.add(3)
+        p_v.add(1)
+        p_q.add(2)
+        p_k.add(2)
+        p_out.add(1)
+        p_v.add(2)
+        take_in()
+        p_q.add(3)
+        p_k.add(3)
+        p_out.add(2)
+        p_v.add(3)
+        p_out.add(3)
+        state["final"].wait()
+        pl.semaphore_wait(credit, 1)
+        for piece in (p_gate, p_up, p_down, *small):
+            for level, copy in piece.copies.items():
+                if level > 0 or piece in (p_k, p_out):
+                    copy.wait_send()
     else:
         for n in range(6):
             results[5][n : n + 1, :] = jnp.sum(sums[n], axis=0, keepdims=True)
-    if plan["fused"]:
-        p_down.add(2)
-        p_gate.add(1)
-        p_down.add(3)
-        share_out()
-        p_up.add(2)
-        p_qk.add(1)
-        p_gate.add(2)
-        p_up.add(3)
-        p_v.add(1)
-        p_qk.add(2)
-        p_gate.add(3)
-        p_out.add(1)
-        p_v.add(2)
-        p_qk.add(3)
-        p_out.add(2)
-        p_v.add(3)
-        p_out.add(3)
-        take_in()
-        state["final"].wait()
-        pl.semaphore_wait(credit, 1)
-        for piece in (p_gate, p_up, p_qk, p_v, p_out, p_down):
-            for level, copy in piece.copies.items():
-                if level > 0 or piece in (p_v, p_out):
-                    copy.wait_send()
-    for copy in (*go_h1, *go_dml, *go_h2, *go_dat, *go_c, *go_d):
+    for copy in (*go_h1, *go_cot, go_row, *go_h2, *go_dat, *go_c, *go_d):
         copy.wait_send()
+
+
+def lay_out_kernel(cuts, whole, ada, tok, out, bias, *refs):
+    (down, gate_up, qkv, wout, ada_to, tok_to, out_to, bias_to) = refs
+    inner, head_cols, pad, own_cols = cuts
+    ada_to[...] = ada[...]
+    tok_to[...] = tok[...]
+    out_to[...] = out[...]
+    down[...] = whole[:, 0:inner]
+    gate_up[:, 0, :] = whole[:, inner : 2 * inner]
+    gate_up[:, 1, :] = whole[:, 2 * inner : 3 * inner]
+    start = 3 * inner
+    for n in range(3):
+        qkv[n] = whole[:, start + n * pad : start + n * pad + head_cols]
+    start += 3 * pad
+    wout[...] = whole[:, start : start + head_cols]
+    bias_to[...] = bias[0:1, 0:own_cols]
+
+
+def lay_out(whole, ada, tok, out, bias, inner, head_cols, own_cols):
+    rows = whole.shape[0]
+    vmem = pl.BlockSpec(memory_space=pltpu.VMEM)
+    pad = -(-head_cols // 128) * 128
+    S = jax.ShapeDtypeStruct
+    return pl.pallas_call(
+        functools.partial(lay_out_kernel, (inner, head_cols, pad, own_cols)),
+        out_shape=(
+            S((rows, inner), F32), S((rows, 2, inner), F32), S((3, rows, head_cols), F32),
+            S((rows, head_cols), F32), S(ada.shape, F32), S(tok.shape, F32), S(out.shape, BF16),
+            S((1, own_cols), F32),
+        ),
+        in_specs=[vmem] * 5,
+        out_specs=[vmem] * 8,
+        compiler_params=pltpu.CompilerParams(vmem_limit_bytes=62 * 1024 * 1024),
+    )(whole, ada, tok, out, bias)
 
 
 def run_block(tok, cot, cond, grid, bias, wada, wqkv, wout, wgu, wdown):
@@ -786,22 +857,23 @@
     hbm = pl.BlockSpec(memory_space=pl.ANY)
     V = pltpu.VMEM
     D = pltpu.SemaphoreType.DMA
-    copies = 8 + 4 * strips
-    fused = count == 16 and width % (8 * count) == 0 and 128 < own_cols <= 256
-    names = ["down", "gate", "up", "qk", "v", "out"]
+    copies = 9 + 4 * strips
+    fused = count == 16 and width % (8 * count) == 0 and 128 < own_cols <= 256 and own_cols % 8 == 0
+    names = ["down", "gate", "up", "q", "k", "v", "out"]
     pad = -(-head_cols // 128) * 128
     if fused:
         results = [
-            jax.ShapeDtypeStruct((width // count, 3 * inner + 2 * head_cols + 2 * pad), F32),
-            jax.ShapeDtypeStruct((width, 256), F32),
+            jax.ShapeDtypeStruct((width // count, 3 * inner + 4 * pad), F32),
+            jax.ShapeDtypeStruct((own_cols, width), F32),
             jax.ShapeDtypeStruct((1, width), F32),
             jax.ShapeDtypeStruct((8, 256), F32),
         ]
         result_specs = [hbm, hbm, vmem, vmem]
         chunk = width // count
-        widths = [inner, inner, inner, 2 * head_cols, pad, pad]
+        widths = [inner, inner, inner, pad, pad, pad, pad]
         extra = [
             V((width // 2, inner), BF16),
+            V((width // 2, pad), BF16),
             V((width // 2, inner), BF16),
             V((chunk, inner), F32),
             D((len(names), 4)),
@@ -829,7 +901,7 @@
     plan = {
         "fused": fused, "results": len(results), "count": count, "pieces": names,
         "devices": devices, "sides": sides, "own_cols": own_cols,
-        "strides": strides, "orders": ((1, 2, 4, 8), (1, 4, 2, 8)),
+        "early": 8, "strides": strides, "orders": ((1, 2, 4, 8), (1, 4, 2, 8)),
     }
     return pl.pallas_call(
         functools.partial(block_kernel, plan),
@@ -842,7 +914,7 @@
         out_specs=[vmem] * 2 + result_specs,
         scratch_shapes=[
             V((8, width), F32), V((2, 16, width // 2), BF16), V((2, HD, LEN), F32),
-            V((2, HD, LEN), F32), V((2, 32, 2, inner), BF16),
+            V((2, HD, LEN), F32), V((3, 48, 2, inner), BF16),
                         V(wqkv.shape, BF16), V(wout.shape, BF16), V((width, inner), BF16),
             V((width, inner), BF16), V(wdown.shape, BF16),
             *[V((2, LEN, width), BF16)] * 4,
@@ -854,10 +926,11 @@
             *[V((2, LEN, inner), BF16)] * 3,
             V((2, 3 * head_cols, LEN), BF16),
             *[V((LEN, width), F32)] * 3,
-            *[V((LEN, width), BF16)] * 5,
+            *[V((LEN, width), BF16)] * 4,
+            *[V((8, width), F32)] * 2,
             V((width, 2 * LEN), BF16),
             V((6, 8, width), F32),
-            D((5,)),
+            D((6,)),
             D((8,)),
             D((copies,)),
             D((copies,)),
@@ -895,21 +968,19 @@
     head_cols = w_out.shape[0]
     wqkv = w_qkv.transpose(1, 2, 0).reshape(3 * head_cols, width)
     layer_out, d_tokens, *grads = run_block(
-        tokens, cotangent, condition, grid_shape, b_ada.reshape(6, width), w_ada, wqkv, w_out,
+        tokens, cotangent, condition, grid_shape, b_ada.reshape(-1, 128), w_ada, wqkv, w_out,
         w_gate_up, w_down,
     )
     devices_all = lax.axis_size("dp") * lax.axis_size("tensor")
     own_cols = 6 * width // devices_all
     if len(grads) == 4:
         whole, ada, d_condition, bias_rows = grads
-        weight_part = ada[:, :own_cols]
-        bias_part = bias_rows[0, :own_cols]
-        pad = -(-head_cols // 128) * 128
-        grad_down = whole[:, :inner].T
-        grad_gate_up = whole[:, inner : 3 * inner].reshape(-1, 2, inner)
-        grad_qkv = whole[:, 3 * inner : 3 * inner + 3 * head_cols].reshape(-1, 3, head_cols)
-        start = 3 * inner + 2 * head_cols + pad
-        grad_out = whole[:, start : start + head_cols].T
+        down, gate_up, qkv, g_out, ada, d_tokens, layer_out, bias_part = lay_out(
+            whole, ada, d_tokens, layer_out, bias_rows, inner, head_cols, own_cols
+        )
+        grad_down, grad_gate_up = down.T, gate_up
+        grad_qkv, grad_out = qkv.transpose(1, 0, 2), g_out.T
+        weight_part, bias_part = ada.T, bias_part.reshape(own_cols)
     else:
         grad_down = sum_over_images(grads[0]).T
         grad_gate_up = jnp.stack([sum_over_images(grads[1]), sum_over_images(grads[2])], axis=1)

time: 217 us -> 183 us (0.84)
  Pallas kernels: 199 us -> 181 us
  local copies, waits for them, and re-layouts: 14.8 us -> 0.6 us
    pallas_call x1, Pallas kernels: 199 us -> 176 us  [run_block(): pl.pallas_call(functools.partial(block_kernel, plan), out_shape=(jax.Shap...]
    pallas_call x0 -> x1, Pallas kernels: none -> 4.67 us  [lay_out(): pl.pallas_call(functools.partial(lay_out_kernel, (inner, head_cols, pad,...]
    unnamed x13 -> x3, local copies, waits for them, and re-layouts: 4.58 us -> 0.6 us
    slice x3 -> x0, local copies, waits for them, and re-layouts: 3.56 us -> none  [the longest x1 1.26 us: body(): bias_part = bias_rows[0, :own_cols]]
    transpose x2 -> x0, local copies, waits for them, and re-layouts: 3.41 us -> none  [the longest x1 1.8 us: body(): grad_down = whole[:, :inner].T]
    reshape x3 -> x0, local copies, waits for them, and re-layouts: 3.29 us -> none  [the longest x1 1.66 us: body(): grad_gate_up = whole[:, inner:3 * inner].reshape(-1, 2, inner)]
where the time goes in v2:
time: 183 us; the launch traced here: 182 us
  Pallas kernels  181 us (99%)
    pallas_call x1, Pallas kernels, run_block(): pl.pallas_call(functools.partial(block_kernel, plan), out_shape=(jax.Shap...  176 us
    pallas_call x1, Pallas kernels, lay_out(): pl.pallas_call(functools.partial(lay_out_kernel, (inner, head_cols, pad,...  4.67 us

profile of v2, /device:TPU:0, one launch (start us, length us, event | category | flops | bytes accessed | tf_op | source)
XLA Modules:
  0.0 182.2 jit_solution(3114812892189110010)
XLA Ops:
  0.6 176.3 %shard_map.169 = (bf16[256,1152]{1,0:T(8,128)(2,1)}, f32[256,1152]{1,0:T(8,128)}, f32[72,7168]{1,0:T(8,128)}, f32[216,1152]{1,0:T(8,128)}, f32[1,1152]{1,0:T(1,128)}, /*index=5*/f32[8,256]{1,0:T(8,128)}) custom-call(bf16[256,1152]{1,0:T(8,128)(2,1)} %tok.1, bf16[256,1152]{1,0:T(8,128)(2,1)} %cot.1, bf16[1,1152]{1,0:T(2,128)(2,1)} %cond.1, s32[2,2]{1,0:T(2,128)} %grid.1, ...), custom_call_target="tpu_custom_call" | custom-call | tf_op jit(solution)/shard_map/pallas_call | solution.py:906
  176.9 0.0 copy-start
  176.9 4.7 %shard_map.170 = (f32[72,1536]{1,0:T(8,128)}, f32[72,2,1536]{2,1,0:T(2,128)}, f32[3,72,576]{2,1,0:T(8,128)}, f32[72,576]{1,0:T(8,128)}, f32[216,1152]{1,0:T(8,12...) custom-call(f32[72,7168]{1,0:T(8,128)} %get-tuple-element.23.whole, ...), custom_call_target="tpu_custom_call" | custom-call | tf_op jit(solution)/shard_map/pallas_call | solution.py:833
  181.6 0.0 copy-done
  181.6 0.6 copy.20
Async XLA Ops:
  176.9 4.7 %copy-start = (f32[1,1152]{1,0:T(1,128)S(1)}, f32[1,1152]{1,0:T(1,128)}, u32[]{:S(2)}) copy-start(f32[1,1152]{1,0:T(1,128)} %get-tuple-element.48) | copy-start | bytes 13828
